TPU v7x, 32 devices: a whole 2x2x4 slice. The times are simulated.
32 devices in a mesh: rows: 16 (over z, y, x), cols: 2 (over core).
Axes of the slice: x: 2, y: 2, z: 4, core: 2. Of those that a mesh axis runs over, the one named last changes fastest.
Arguments:
- fields: bfloat16 [6144, 512], P('rows', 'cols'), may hold values from -6 to 6
- masks: int32 [6144, 512], P('rows', 'cols'), may hold values from 1 to 256
- offsets: int32 [16, 2], P('rows', 'cols'), may hold values from 0 to 127
Outputs:
- stitched: float32 [4096, 512], P('rows', 'cols')
Inputs may be any that keep to these rules, and one draw needn't show every extreme that they name: `offsets`: row offset of a field below its tile's first row.
All inputs are finite; a program needn't handle non-finite values.
Results may differ from a plain program's by a relative error of at most 0.0003.
Values sent between devices are 32-bit elements; how exact they have to be, the bound alone decides.
A program may use at most 64 MiB of HBM per device.

v0:
```python
import math

import jax
import jax.numpy as jnp
from jax import lax
from jax.sharding import PartitionSpec as P

MARGIN = 128


highest = lax.Precision.HIGHEST


def shifted(block, axis, distance):
    devices = range(lax.axis_size(axis))
    route = [(i - distance, i) for i in devices if i - distance in devices]
    return lax.ppermute(block, axis, route)


def cosine_table(waves, positions, length):
    phase_index = (2 * positions + 1) * waves % (4 * length)
    cosines = jnp.cos(phase_index.astype(jnp.float32) * (math.pi / (2 * length)))
    normalizer = jnp.where(waves == 0, math.sqrt(1.0 / length), math.sqrt(2.0 / length))
    return cosines * normalizer


def exact_product(left, right):
    return jnp.dot(left, right, precision=highest, preferred_element_type=jnp.float32)


def phase_pair(first, second, modulus):
    phase_index = first[:, None] * second[None, :] % modulus
    angles = phase_index.astype(jnp.float32) * (2.0 * math.pi / modulus)
    return (jnp.cos(angles), jnp.sin(angles))


def strip_forward(values):
    held_count, length = values.shape
    outer_len = math.gcd(length, 128)
    inner_len = length // outer_len
    evens = values[:, 0::2]
    odds = values[:, 1::2][:, ::-1]
    reordered = jnp.concatenate([evens, odds], axis=1).reshape(held_count, outer_len, inner_len)
    outer_iota = lax.iota(jnp.int32, outer_len)
    inner_iota = lax.iota(jnp.int32, inner_len)
    cos_outer, sin_outer = phase_pair(outer_iota, outer_iota, outer_len)
    real_one = jnp.einsum("kn,hnm->hkm", cos_outer, reordered, precision=highest)
    imag_one = -jnp.einsum("kn,hnm->hkm", sin_outer, reordered, precision=highest)
    cos_twist, sin_twist = phase_pair(outer_iota, inner_iota, length)
    real_two = real_one * cos_twist + imag_one * sin_twist
    imag_two = imag_one * cos_twist - real_one * sin_twist
    cos_inner, sin_inner = phase_pair(inner_iota, inner_iota, inner_len)
    real_three = jnp.einsum("hkm,mq->hkq", real_two, cos_inner, precision=highest) + jnp.einsum(
        "hkm,mq->hkq", imag_two, sin_inner, precision=highest
    )
    imag_three = jnp.einsum("hkm,mq->hkq", imag_two, cos_inner, precision=highest) - jnp.einsum(
        "hkm,mq->hkq", real_two, sin_inner, precision=highest
    )
    real_full = real_three.transpose(0, 2, 1).reshape(held_count, length)
    imag_full = imag_three.transpose(0, 2, 1).reshape(held_count, length)
    waves = lax.iota(jnp.int32, length)
    turn = waves.astype(jnp.float32) * (math.pi / (2 * length))
    normalizer = jnp.where(waves == 0, math.sqrt(1.0 / length), math.sqrt(2.0 / length))
    return normalizer * (jnp.cos(turn) * real_full + jnp.sin(turn) * imag_full)


def strip_inverse(coefficients):
    _, pullback = jax.vjp(strip_forward, jnp.zeros_like(coefficients))
    return pullback(coefficients)[0]


def shards(fields, masks, offsets):
    tile_rows = fields.shape[0] - MARGIN
    tile_cols = fields.shape[1]
    strip_rows = tile_rows * lax.axis_size("rows")
    strip_cols = tile_cols * lax.axis_size("cols")
    screen = 16.0 / (tile_cols * tile_cols)
    picture = fields.astype(jnp.float32)
    weight = masks.astype(jnp.float32)
    downward = jnp.concatenate(
        [picture[1:] - picture[:-1], jnp.zeros((1, tile_cols), jnp.float32)], axis=0
    )
    across = jnp.concatenate(
        [picture[:, 1:] - picture[:, :-1], jnp.zeros((picture.shape[0], 1), jnp.float32)], axis=1
    )
    stacked = jnp.stack([weight, weight * picture, weight * downward, weight * across])
    canvas = jnp.zeros((4, tile_rows + 2 * MARGIN, tile_cols), jnp.float32)
    canvas = lax.dynamic_update_slice(canvas, stacked, (jnp.int32(0), offsets[0, 0], jnp.int32(0)))
    spillage = lax.slice_in_dim(canvas, tile_rows, tile_rows + 2 * MARGIN, axis=1)
    arrived = shifted(spillage, "rows", 1)
    incoming = arrived[:, : 2 * MARGIN - 1]
    totals = canvas[:, :tile_rows].at[:, : 2 * MARGIN - 1].add(incoming)
    divisor = jnp.maximum(totals[0], 1.0)
    composite = totals[1] / divisor
    row_global = lax.axis_index("rows") * tile_rows + lax.iota(jnp.int32, tile_rows)
    grad_rows = jnp.where((row_global == strip_rows - 1)[:, None], 0.0, totals[2] / divisor)
    grad_cols = totals[3] / divisor
    upper_row = shifted(grad_rows[-1], "rows", 1)
    rows_before = jnp.concatenate([upper_row[None, :], grad_rows[:-1]], axis=0)
    cols_before = jnp.concatenate(
        [jnp.zeros((tile_rows, 1), jnp.float32), grad_cols[:, :-1]], axis=1
    )
    divergence = grad_rows - rows_before + (grad_cols - cols_before)
    right_side = screen * composite - divergence
    col_base = lax.axis_index("cols") * tile_cols
    own_cols = col_base + lax.iota(jnp.int32, tile_cols)
    every_col = lax.iota(jnp.int32, strip_cols)
    all_waves_table = cosine_table(every_col[:, None], own_cols[None, :], strip_cols)
    own_waves_table = cosine_table(own_cols[:, None], every_col[None, :], strip_cols)
    right_flipped = right_side.T
    spectral = lax.psum_scatter(
        exact_product(all_waves_table, right_flipped), "cols", scatter_dimension=0, tiled=True
    )
    held_data = lax.all_to_all(spectral, "rows", split_axis=0, concat_axis=1, tiled=True)
    held_count = held_data.shape[0]
    coefficients = strip_forward(held_data)
    row_eigen = 4.0 * jnp.square(
        jnp.sin(lax.iota(jnp.float32, strip_rows) * (math.pi / (2 * strip_rows)))
    )
    held_waves = col_base + lax.axis_index("rows") * held_count + lax.iota(jnp.int32, held_count)
    col_eigen = 4.0 * jnp.square(
        jnp.sin(held_waves.astype(jnp.float32) * (math.pi / (2 * strip_cols)))
    )
    denominator = screen + row_eigen[None, :] + col_eigen[:, None]
    quotient = coefficients / denominator
    restored = strip_inverse(quotient)
    returned = lax.all_to_all(restored, "rows", split_axis=1, concat_axis=0, tiled=True)
    solved = lax.psum_scatter(
        exact_product(own_waves_table.T, returned), "cols", scatter_dimension=0, tiled=True
    )
    return solved.T


def solution(mesh):
    placed = (P("rows", "cols"), P("rows", "cols"), P("rows", "cols"))
    return jax.shard_map(
        shards, mesh=mesh, in_specs=placed, out_specs=P("rows", "cols"), check_vma=False
    )
```

profile of v0, /device:TPU:0, one launch (start us, length us, event | category | flops | bytes accessed | tf_op | source)
XLA Modules:
  0.0 155.9 jit_solution(3623632662777125258)
XLA Ops:
  6.5 1.0 convert_element_type.97
  8.6 1.3 pad_maximum_fusion
  10.1 8.3 %dynamic_update_slice.3 = f32[4,512,256]{2,1,0:T(8,128)S(1)} dynamic-update-slice(f32[4,512,256]{2,1,0:T(8,128)S(1)} %broadcast_in_dim.48, f32[4,384,256]{2,1,0:T(8,128)} %pad_maximum_fusion, s32[]{:T(128)} %constant.138.clone.1, s32[]{:T(128)S(6)} %select_n.122, s32[]{:T(128)} %constant.138.clone.1) | dynamic-update-slice | bytes 3145732 | tf_op jit(solution)/shard_map/dynamic_update_slice | solution.py:88
  18.4 1.2 fusion.207
  19.6 5.3 %collective-permute-start = (f32[4,256,256]{2,1,0:T(8,128)S(1)}, f32[4,256,256]{2,1,0:T(8,128)}, u32[]{:S(2)}, u32[]{:S(2)}) collective-permute-start(f32[4,256,256]{2,1,0:T(8,128)S(1)} %get-tuple-element.17), channel_id=1, source_target_pairs={{0,2},{2,4},{4,6},{6,8},{8,10},{10,12},{12,14},{14,16},{16,18},{18... | collective-permute-start | bytes 3145736 | tf_op jit(solution)/shard_map/ppermute | solution.py:17
  24.9 21.6 %collective-permute-done = f32[4,256,256]{2,1,0:T(8,128)} collective-permute-done((f32[4,256,256]{2,1,0:T(8,128)S(1)}, f32[4,256,256]{2,1,0:T(8,128)}, u32[]{:S(2)}, u32[]{:S(2)}) %collective-permute-start) | collective-permute-done | bytes 1048608 | tf_op jit(solution)/shard_map/ppermute | solution.py:17
  46.5 1.4 slice_add_fusion
  47.9 5.1 %scatter-add.4 = f32[4,256,256]{2,1,0:T(8,128)} dynamic-update-slice(f32[4,256,256]{2,1,0:T(8,128)} %get-tuple-element.18, f32[4,255,256]{2,1,0:T(8,128)S(1)} %slice_add_fusion, s32[]{:T(128)} %constant.138.clone.1, s32[]{:T(128)} %constant.138.clone.1, s32[]{:T(128)} %constant.138.clone.1) | dynamic-update-slice | bytes 2088964 | tf_op jit(solution)/shard_map/scatter-add | solution.py:92
  53.0 1.1 fusion.34
  54.1 4.5 %collective-permute-start.1 = (f32[256]{0:T(256)S(1)}, f32[256]{0:T(256)S(1)}, u32[]{:S(2)}, u32[]{:S(2)}) collective-permute-start(f32[256]{0:T(256)S(1)} %bitcast.93), channel_id=1, source_target_pairs={{0,2},{2,4},{4,6},{6,8},{8,10},{10,12},{12,14},{14,16},{16,18},{18... | collective-permute-start | bytes 3080 | tf_op jit(solution)/shard_map/ppermute | solution.py:17
  58.6 1.1 fusion.32
  59.9 4.5 %fusion.21 = f32[512,256]{1,0:T(8,128)} fusion(f32[4,256,256]{2,1,0:T(8,128)} %scatter-add.4, f32[256,256]{1,0:T(8,128)S(1)} %fusion.34, f32[255,256]{1,0:T(8,128)S(1)} %bitcast.88, f32[1,256]{1,0:T(1,128)S(1)} %bitcast.94, f32[256,256]{1,0:T(8,128)S(1)} %fusion.32, f32[256,255]{1,0:T(8,128)S(1)} %bitcast.89, f32[512]{0:T(512)S(1)} %fusion.146, ...), kind=kOutput, calls=%fused_computation.37 | convolution fusion | flops 405143552 | bytes 2099200 | tf_op jit(solution)/shard_map/dot_general | solution.py:28
  64.5 12.0 %reduce-scatter.3.cloned.1.call-done = f32[256,256]{1,0:T(8,128)} async-done(((f32[512,256]{1,0:T(8,128)}), f32[256,256]{1,0:T(8,128)}) %reduce-scatter.3.cloned.1.call-update) | async-done | bytes 262160 | tf_op jit(solution)/shard_map/reduce_scatter | solution.py:111
  76.5 6.8 %all-to-all-start = ((f32[16,16,256]{2,1,0:T(8,128)}), f32[16,16,256]{2,1,0:T(8,128)S(1)}, u32[]{:S(2)}, u32[]{:S(2)}) async-start(f32[16,16,256]{2,1,0:T(8,128)} %bitcast.90), calls=%async_computation.1 | async-start | bytes 524288 | tf_op jit(solution)/shard_map/all_to_all | solution.py:114
  83.7 10.0 %all-to-all-done = f32[16,16,256]{2,1,0:T(8,128)S(1)} async-done(((f32[16,16,256]{2,1,0:T(8,128)}), f32[16,16,256]{2,1,0:T(8,128)S(1)}, u32[]{:S(2)}, u32[]{:S(2)}) %all-to-all-start) | async-done | bytes 262176 | tf_op jit(solution)/shard_map/all_to_all | solution.py:114
  93.7 4.4 %slice.89 = f32[16,2048]{1,0:T(8,128)S(1)} slice(f32[16,4096]{1,0:T(8,128)S(1)} %bitcast.86), slice={[0:16:1], [1:4096:2]} | slice | bytes 262144 | tf_op jit(solution)/shard_map/slice | solution.py:42
  98.0 4.4 %slice.88 = f32[16,2048]{1,0:T(8,128)S(1)} slice(f32[16,4096]{1,0:T(8,128)S(1)} %bitcast.87), slice={[0:16:1], [0:4096:2]} | slice | bytes 262144 | tf_op jit(solution)/shard_map/slice | solution.py:41
  102.4 1.3 rev.6
  104.1 1.8 %convolution_bitcast_fusion = f32[16,128,32]{1,2,0:T(8,128)S(1)} fusion(f32[16,128,32]{2,1,0:T(8,128)S(1)} %reshape.230), kind=kOutput, calls=%fused_computation.14 | convolution fusion | flops 100892672 | bytes 524288 | tf_op jit(solution)/shard_map/kn,hnm->hkm/dot_general | solution.py:47
  105.9 1.8 %fusion.6 = f32[16,128,32]{1,2,0:T(8,128)S(1)} fusion(f32[16,128,32]{2,1,0:T(8,128)S(1)} %reshape.230), kind=kOutput, calls=%fused_computation.13 | convolution fusion | flops 100958208 | bytes 524288 | tf_op jit(solution)/shard_map/kn,hnm->hkm/dot_general | solution.py:48
  109.1 0.6 fusion.9
  111.6 0.6 fusion.47
  112.2 0.6 fusion
  113.7 1.3 rev.7
  115.0 4.3 %pad.11 = f32[16,4096]{1,0:T(8,128)S(1)} pad(f32[16,2048]{1,0:T(8,128)S(1)} %rev.7, f32[]{:T(128)} %constant.148.clone.1), padding=0_0_0x1_0_1 | pad | bytes 393220 | tf_op jit(solution)/shard_map/transpose(jvp())/pad | solution.py:42
  119.4 4.4 %pad.12 = f32[16,4096]{1,0:T(8,128)S(1)} pad(f32[16,2048]{1,0:T(8,128)S(1)} %get-tuple-element.22, f32[]{:T(128)} %constant.148.clone.1), padding=0_0_0x0_1_1 | pad | bytes 393220 | tf_op jit(solution)/shard_map/transpose(jvp())/pad | solution.py:41
  123.8 0.7 copy.42
  124.5 3.5 %all-to-all-start.1 = ((f32[16,16,256]{2,0,1:T(8,128)}), f32[16,16,256]{2,0,1:T(8,128)S(1)}, u32[]{:S(2)}, u32[]{:S(2)}) async-start(f32[16,16,256]{2,0,1:T(8,128)} %bitcast.78), calls=%async_computation.2 | async-start | bytes 524288 | tf_op jit(solution)/shard_map/all_to_all | solution.py:127
  128.1 9.4 %all-to-all-done.1 = f32[16,16,256]{2,0,1:T(8,128)S(1)} async-done(((f32[16,16,256]{2,0,1:T(8,128)}), f32[16,16,256]{2,0,1:T(8,128)S(1)}, u32[]{:S(2)}, u32[]{:S(2)}) %all-to-all-start.1) | async-done | bytes 262176 | tf_op jit(solution)/shard_map/all_to_all | solution.py:127
  137.5 3.6 %fusion.14 = f32[512,256]{1,0:T(8,128)} fusion(f32[256,256]{1,0:T(8,128)S(1)} %bitcast.91, f32[256]{0:T(256)S(1)} %compare_select_fusion, s32[256]{0:T(256)S(1)} %iota_add_fusion, s32[512]{0:T(512)S(1)} %multiply_add_fusion.5), kind=kOutput, calls=%fused_computation.31 | convolution fusion | flops 404619264 | bytes 790528 | tf_op jit(solution)/shard_map/dot_general | solution.py:28
  141.2 6.0 %reduce-scatter.5.cloned.1.call-done = f32[256,256]{1,0:T(8,128)} async-done(((f32[512,256]{1,0:T(8,128)}), f32[256,256]{1,0:T(8,128)}) %reduce-scatter.5.cloned.1.call-update) | async-done | bytes 262160 | tf_op jit(solution)/shard_map/reduce_scatter | solution.py:128
  147.2 1.8 %copy.28 = f32[256,256]{1,0:T(8,128)} copy(f32[256,256]{0,1:T(8,128)} %bitcast.92) | data formatting | bytes 524288 | tf_op jit(solution)/shard_map/transpose | solution.py:131
  (41 shorter events, 5.9 us)
Async XLA Ops:
  6.5 1.2 copy-start
  6.5 70.0 %reduce-scatter.3.cloned.1.call-start = ((), (), s32[]{:S(2)}) async-start(), calls=%async_computation.4 | async-start | bytes 786432 | tf_op jit(solution)/shard_map/reduce_scatter | solution.py:111
  7.5 0.9 copy-start.1
  19.6 26.9 %collective-permute-start = (f32[4,256,256]{2,1,0:T(8,128)S(1)}, f32[4,256,256]{2,1,0:T(8,128)}, u32[]{:S(2)}, u32[]{:S(2)}) collective-permute-start(f32[4,256,256]{2,1,0:T(8,128)S(1)} %get-tuple-element.17), channel_id=1, source_target_pairs={{0,2},{2,4},{4,6},{6,8},{8,10},{10,12},{12,14},{14,16},{16,18},{18... | collective-permute-start | bytes 3145736 | tf_op jit(solution)/shard_map/ppermute | solution.py:17
  54.1 5.8 %collective-permute-start.1 = (f32[256]{0:T(256)S(1)}, f32[256]{0:T(256)S(1)}, u32[]{:S(2)}, u32[]{:S(2)}) collective-permute-start(f32[256]{0:T(256)S(1)} %bitcast.93), channel_id=1, source_target_pairs={{0,2},{2,4},{4,6},{6,8},{8,10},{10,12},{12,14},{14,16},{16,18},{18... | collective-permute-start | bytes 3080 | tf_op jit(solution)/shard_map/ppermute | solution.py:17
  76.5 17.1 %all-to-all-start = ((f32[16,16,256]{2,1,0:T(8,128)}), f32[16,16,256]{2,1,0:T(8,128)S(1)}, u32[]{:S(2)}, u32[]{:S(2)}) async-start(f32[16,16,256]{2,1,0:T(8,128)} %bitcast.90), calls=%async_computation.1 | async-start | bytes 524288 | tf_op jit(solution)/shard_map/all_to_all | solution.py:114
  124.5 13.0 %all-to-all-start.1 = ((f32[16,16,256]{2,0,1:T(8,128)}), f32[16,16,256]{2,0,1:T(8,128)S(1)}, u32[]{:S(2)}, u32[]{:S(2)}) async-start(f32[16,16,256]{2,0,1:T(8,128)} %bitcast.78), calls=%async_computation.2 | async-start | bytes 524288 | tf_op jit(solution)/shard_map/all_to_all | solution.py:127
  128.1 19.2 %reduce-scatter.5.cloned.1.call-start = ((), (), s32[]{:S(2)}) async-start(), calls=%async_computation.5 | async-start | bytes 786432 | tf_op jit(solution)/shard_map/reduce_scatter | solution.py:128
Sparse Core Ops, SparseCore 0:
  64.5 11.9 reduce-scatter.2
  141.3 5.8 reduce-scatter.4
where the time goes:
time: 157 us; the launch traced here: 156 us
  waiting for transfers between devices  59.3 us (38%)
  local copies, waits for them, and re-layouts  38.6 us (25%)
  starting transfers between devices  20.1 us (13%)
  matrix products  16.8 us (11%)
  between operations  14.4 us (9%)
  other arithmetic  6.7 us (4%)
    ppermute x2, waiting for transfers between devices, shifted(): return lax.ppermute(block, axis, route)  21.8 us
    reduce_scatter x1, waiting for transfers between devices, shards(): lax.psum_scatter(exact_product(all_waves_table, right_flipped), 'cols', s...  12 us
    all_to_all x1, waiting for transfers between devices, shards(): lax.all_to_all(spectral, 'rows', split_axis=0, concat_axis=1, tiled=True)  9.97 us
    ppermute x2, starting transfers between devices, shifted(): return lax.ppermute(block, axis, route)  9.79 us
    all_to_all x1, waiting for transfers between devices, shards(): lax.all_to_all(restored, 'rows', split_axis=1, concat_axis=0, tiled=True)  9.4 us
    dynamic_update_slice x1, local copies, waits for them, and re-layouts, shards(): lax.dynamic_update_slice(canvas, stacked, (jnp.int32(0), offsets[0, 0], j...  8.32 us
    dot_general x2, matrix products, exact_product(): jnp.dot(left, right, precision=highest, preferred_element_type=jnp.float32)  8.12 us
    all_to_all x1, starting transfers between devices, shards(): lax.all_to_all(spectral, 'rows', split_axis=0, concat_axis=1, tiled=True)  6.76 us
  transfers between devices with their start and end apart: 6, of which 6 were waited for; matrix products, arithmetic and copies ran while one was open for 1% of the time, Pallas kernels for 0%

commit v1 on v0

v1 whole, which is shorter than its diff:
```python
import functools
import math

import jax
import jax.numpy as jnp
import numpy as np
from jax import lax
from jax.experimental import pallas as pl
from jax.experimental.pallas import tpu as pltpu
from jax.sharding import PartitionSpec as P

MARGIN = 128
MESH = pl.DeviceIdType.MESH
HIGHEST = lax.Precision.HIGHEST


def cosine_matrix(length):
    k = np.arange(length)[:, None]
    i = np.arange(length)[None, :]
    table = np.cos(np.pi * (((2 * i + 1) * k) % (4 * length)) / (2 * length))
    table *= np.where(k == 0, math.sqrt(1.0 / length), math.sqrt(2.0 / length))
    return table


def make_tables(n, tile_cols, n_rows, n_cols):
    strip_cols = n_cols * tile_cols
    screen = 16.0 / (tile_cols * tile_cols)
    full = cosine_matrix(strip_cols)
    blocks = full.reshape(n_cols, tile_cols, n_cols, tile_cols)
    inverse = blocks.transpose(2, 0, 1, 3)
    forward = blocks.transpose(0, 2, 3, 1)
    local = cosine_matrix(n)
    row_eigen = 4.0 * np.sin(np.pi * np.arange(n) / (2 * n)) ** 2
    col_eigen = 4.0 * np.sin(np.pi * np.arange(strip_cols) / (2 * strip_cols)) ** 2
    mu = screen + col_eigen
    theta = 2.0 * np.arcsinh(np.sqrt(mu) / 2.0)
    edge = np.exp(-theta) / (2.0 * np.sinh(theta))
    q = np.exp(-n * theta)
    params = np.zeros((n_cols, 8, tile_cols))
    params[:, 0] = theta.reshape(n_cols, tile_cols)
    params[:, 1] = (n * theta).reshape(n_cols, tile_cols)
    params[:, 2] = (edge / (1.0 - q ** (2 * n_rows))).reshape(n_cols, tile_cols)
    params[:, 3] = (edge / (1.0 - q * q)).reshape(n_cols, tile_cols)
    params[:, 4] = (edge * q / (1.0 - q * q)).reshape(n_cols, tile_cols)
    params[:, 5] = mu.reshape(n_cols, tile_cols)
    eigen = np.broadcast_to(row_eigen[:, None], (n, 128))
    return [np.ascontiguousarray(t, dtype=np.float32) for t in (forward, inverse, local, local.T, eigen, params)]


def exact(left, right):
    return jnp.dot(left, right, precision=HIGHEST, preferred_element_type=jnp.float32)


def kernel(
    n_rows, n_cols, off_ref, f_ref, m_ref, fwd_hbm, inv_hbm, loc_ref, loct_ref, eig_ref, par_ref,
    out_ref, spill_out, spill_in, xs, ys, mom, fwd, inv, local_t, wave_f, wave_b,
    spill_sem, x_send, x_recv, y_send, y_recv, m_send, m_recv, tab_sem,
):
    a = lax.axis_index("rows")
    b = lax.axis_index("cols")
    n, w = out_ref.shape
    screen = 16.0 / (w * w)

    barrier = pltpu.get_barrier_semaphore()
    for k in range(1, n_rows):
        pl.semaphore_signal(barrier, inc=1, device_id={"rows": lax.rem(a + k, n_rows)}, device_id_type=MESH)
    for k in range(1, n_cols):
        pl.semaphore_signal(barrier, inc=1, device_id={"cols": lax.rem(b + k, n_cols)}, device_id_type=MESH)
    load_fwd = pltpu.make_async_copy(fwd_hbm.at[b], fwd, tab_sem.at[0])
    load_inv = pltpu.make_async_copy(inv_hbm.at[b], inv, tab_sem.at[1])
    load_fwd.start()
    load_inv.start()

    s = off_ref[0, 0]
    height = f_ref.shape[0]
    pair = jnp.concatenate(
        [f_ref[...], m_ref[...].astype(jnp.float32).astype(jnp.bfloat16)], axis=1
    )
    r_at = lax.broadcasted_iota(jnp.int32, (n, height), 0)
    t_at = lax.broadcasted_iota(jnp.int32, (n, height), 1) + s
    one_below = jnp.where(r_at + n == t_at, 1.0, 0.0).astype(jnp.bfloat16)
    one_own = jnp.where(r_at == t_at, 1.0, 0.0).astype(jnp.bfloat16)
    below = jnp.dot(one_below, pair, preferred_element_type=jnp.float32)
    own = jnp.dot(one_own, pair, preferred_element_type=jnp.float32)
    f1 = own[:, :w]
    m1 = own[:, w:]
    row_at = lax.broadcasted_iota(jnp.int32, (n, w), 0)
    col_at = lax.broadcasted_iota(jnp.int32, (n, w), 1)
    last_row = row_at == n - 1
    last_col = col_at == w - 1
    next_f = below[0:1, :w]
    m_end = m1[n - 1 : n]
    g_end = m_end * (next_f - f1[n - 1 : n]) / jnp.maximum(m_end, 1.0)
    spill_out[:, :w] = jnp.where(last_row, g_end, below[:, :w])
    spill_out[:, w:] = below[:, w:]

    pl.semaphore_wait(barrier, n_rows - 1 + n_cols - 1)
    spill_copy = pltpu.make_async_remote_copy(
        src_ref=spill_out, dst_ref=spill_in, send_sem=spill_sem.at[0], recv_sem=spill_sem.at[1],
        device_id={"rows": lax.rem(a + 1, n_rows)}, device_id_type=MESH,
    )

    @pl.when(a < n_rows - 1)
    def _():
        spill_copy.start()

    f1_next = jnp.where(last_row, next_f, pltpu.roll(f1, n - 1, 0))
    p1 = m1 * f1
    sx1 = m1 * (f1_next - f1)
    sy1 = m1 * jnp.where(last_col, 0.0, pltpu.roll(f1, w - 1, 1) - f1)
    theta = par_ref[b, 0:1]
    n_theta = par_ref[b, 1:2]
    wide_edge = par_ref[b, 2:3]
    tile_edge = par_ref[b, 3:4]
    tile_edge_q = par_ref[b, 4:5]
    mu = par_ref[b, 5:6]
    row_f = row_at.astype(jnp.float32)
    wave_b[...] = jnp.exp(-theta * row_f)
    wave_f[...] = jnp.exp(-theta * ((n - 1) - row_f))

    @pl.when(a == 0)
    def _():
        spill_in[...] = jnp.zeros_like(spill_in)

    @pl.when(a > 0)
    def _():
        spill_copy.wait_recv()

    f2 = spill_in[:, :w]
    m2 = spill_in[:, w:]
    m2_next = pltpu.roll(m2, n - 1, 0)
    down2 = jnp.where(m2_next > 0.0, pltpu.roll(f2, n - 1, 0) - f2, 0.0)
    across2 = jnp.where(last_col, 0.0, pltpu.roll(f2, w - 1, 1) - f2)
    scale = 1.0 / jnp.maximum(m1 + m2, 1.0)
    composite = (p1 + m2 * f2) * scale
    gx = (sx1 + m2 * down2) * scale
    gx = jnp.where(last_row & (a == n_rows - 1), 0.0, gx)
    gy = (sy1 + m2 * across2) * scale
    gx_before = jnp.where(row_at == 0, spill_in[n - 1 : n, :w], pltpu.roll(gx, 1, 0))
    gy_before = jnp.where(col_at == 0, 0.0, pltpu.roll(gy, 1, 1))
    xs[b] = screen * composite - ((gx - gx_before) + (gy - gy_before))

    def swap(buf, send, recv):
        copies = []
        for k in range(1, n_cols):
            to = lax.rem(b + k, n_cols)
            copies.append(
                pltpu.make_async_remote_copy(
                    src_ref=buf.at[b], dst_ref=buf.at[b], send_sem=send.at[k], recv_sem=recv.at[k],
                    device_id={"cols": to}, device_id_type=MESH,
                )
            )
            copies[-1].start()
        return copies

    def gathered(buf, copies, table):
        total = exact(buf[b], table[b])
        for k in range(1, n_cols):
            copies[k - 1].wait_recv()
            at = lax.rem(b + n_cols - k, n_cols)
            total += exact(buf[at], table[at])
        return total

    x_copies = swap(xs, x_send, x_recv)
    load_fwd.wait()
    spectral = gathered(xs, x_copies, fwd)

    mom_f = jnp.sum(wave_f[...] * spectral, axis=0, keepdims=True)
    mom_b = jnp.sum(wave_b[...] * spectral, axis=0, keepdims=True)
    sub = lax.broadcasted_iota(jnp.int32, (8, w), 0)
    mom[a] = jnp.where(sub == 0, mom_f, jnp.where(sub == 1, mom_b, 0.0))
    m_copies = []
    for k in range(1, n_rows):
        m_copies.append(
            pltpu.make_async_remote_copy(
                src_ref=mom.at[a], dst_ref=mom.at[a], send_sem=m_send.at[k], recv_sem=m_recv.at[k],
                device_id={"rows": lax.rem(a + k, n_rows)}, device_id_type=MESH,
            )
        )
        m_copies[-1].start()
    eig = jnp.concatenate([eig_ref[...]] * (w // 128), axis=1)
    quotient = exact(loc_ref[...], spectral) / (eig + mu)
    local_t[...] = exact(loct_ref[...], quotient)
    for copy in m_copies:
        copy.wait_recv()
    period = 2 * n_rows
    top = jnp.zeros((8, w), jnp.float32)
    bottom = jnp.zeros((8, w), jnp.float32)
    for other in range(n_rows):
        e_top = jnp.where(sub == 0, lax.rem(a - 1 - other + period, period), a + other)
        e_bottom = jnp.where(sub == 0, period - 2 - a - other, lax.rem(other - a - 1 + period, period))
        held = mom[other]
        top += jnp.exp(-n_theta * e_top.astype(jnp.float32)) * held
        bottom += jnp.exp(-n_theta * e_bottom.astype(jnp.float32)) * held
    from_top = wide_edge * jnp.sum(top, axis=0, keepdims=True) - (tile_edge * mom_b + tile_edge_q * mom_f)
    from_bottom = wide_edge * jnp.sum(bottom, axis=0, keepdims=True) - (tile_edge * mom_f + tile_edge_q * mom_b)
    ys[b] = local_t[...] + wave_b[...] * from_top + wave_f[...] * from_bottom

    y_copies = swap(ys, y_send, y_recv)
    load_inv.wait()
    out_ref[...] = gathered(ys, y_copies, inv)

    for copy in x_copies + y_copies + m_copies:
        copy.wait_send()

    @pl.when(a < n_rows - 1)
    def _():
        spill_copy.wait_send()


def shards(n_rows, n_cols, fields, masks, offsets):
    n = fields.shape[0] - MARGIN
    w = fields.shape[1]
    tables = make_tables(n, w, n_rows, n_cols)
    vmem = pl.BlockSpec(memory_space=pltpu.VMEM)
    anywhere = pl.BlockSpec(memory_space=pl.ANY)
    f32 = jnp.float32
    return pl.pallas_call(
        functools.partial(kernel, n_rows, n_cols),
        out_shape=jax.ShapeDtypeStruct((n, w), f32),
        in_specs=[pl.BlockSpec(memory_space=pltpu.SMEM), vmem, vmem, anywhere, anywhere] + [vmem] * 4,
        out_specs=vmem,
        scratch_shapes=[
            pltpu.VMEM((n, 2 * w), f32),
            pltpu.VMEM((n, 2 * w), f32),
            pltpu.VMEM((n_cols, n, w), f32),
            pltpu.VMEM((n_cols, n, w), f32),
            pltpu.VMEM((n_rows, 8, w), f32),
            pltpu.VMEM((n_cols, w, w), f32),
            pltpu.VMEM((n_cols, w, w), f32),
            pltpu.VMEM((n, w), f32),
            pltpu.VMEM((n, w), f32),
            pltpu.VMEM((n, w), f32),
            pltpu.SemaphoreType.DMA((2,)),
            pltpu.SemaphoreType.DMA((n_cols,)),
            pltpu.SemaphoreType.DMA((n_cols,)),
            pltpu.SemaphoreType.DMA((n_cols,)),
            pltpu.SemaphoreType.DMA((n_cols,)),
            pltpu.SemaphoreType.DMA((n_rows,)),
            pltpu.SemaphoreType.DMA((n_rows,)),
            pltpu.SemaphoreType.DMA((2,)),
        ],
        compiler_params=pltpu.CompilerParams(
            collective_id=0, has_side_effects=True, vmem_limit_bytes=56 * 1024 * 1024
        ),
    )(offsets, fields, masks, *tables)


def solution(mesh):
    placed = (P("rows", "cols"), P("rows", "cols"), P("rows", "cols"))
    body = functools.partial(shards, mesh.shape["rows"], mesh.shape["cols"])
    return jax.shard_map(body, mesh=mesh, in_specs=placed, out_specs=P("rows", "cols"), check_vma=False)
```

time: 157 us -> 32 us (0.20)
  waiting for transfers between devices: 59.3 us -> 0 us
  local copies, waits for them, and re-layouts: 38.6 us -> 1.67 us
  Pallas kernels: 0 us -> 29.5 us
  starting transfers between devices: 20.1 us -> 0 us
  matrix products: 16.8 us -> 0 us
  between operations: 14.4 us -> 0.66 us
  other arithmetic: 6.7 us -> 0 us
    pallas_call x0 -> x1, Pallas kernels: none -> 29.5 us  [shards(): pl.pallas_call(functools.partial(kernel, n_rows, n_cols), out_shape=jax.S...]
    ppermute x2 -> x0, waiting for transfers between devices: 21.8 us -> none  [shifted(): return lax.ppermute(block, axis, route)]
    all_to_all x2 -> x0, waiting for transfers between devices: 19.4 us -> none  [the longest x1 9.97 us: shards(): lax.all_to_all(spectral, 'rows', split_axis=0, concat_axis=1, tiled=True)]
    reduce_scatter x2 -> x0, waiting for transfers between devices: 18 us -> none  [the longest x1 12 us: shards(): lax.psum_scatter(exact_product(all_waves_table, right_flipped), 'cols', s...]
    dot_general x14 -> x0, matrix products: 16.8 us -> none  [the longest x2 8.12 us: exact_product(): jnp.dot(left, right, precision=highest, preferred_element_type=jnp.float32)]
    all_to_all x2 -> x0, starting transfers between devices: 10.3 us -> none  [the longest x1 6.76 us: shards(): lax.all_to_all(spectral, 'rows', split_axis=0, concat_axis=1, tiled=True)]
    slice x4 -> x0, local copies, waits for them, and re-layouts: 9.9 us -> none  [the longest x1 4.36 us: strip_forward(): evens = values[:, 0::2]]
    ppermute x2 -> x0, starting transfers between devices: 9.79 us -> none  [shifted(): return lax.ppermute(block, axis, route)]
  transfers between devices with their start and end apart: 6 -> 0, of which waited for: 6 -> 0; matrix products, arithmetic and copies ran while one was open for 1% -> 0% of each run, Pallas kernels for 0% -> 0%
where the time goes in v1:
time: 32 us; the launch traced here: 31.8 us
  Pallas kernels  29.5 us (92%)
  local copies, waits for them, and re-layouts  1.67 us (5%)
  between operations  0.66 us (2%)
    pallas_call x1, Pallas kernels, shards(): pl.pallas_call(functools.partial(kernel, n_rows, n_cols), out_shape=jax.S...  29.5 us
    unnamed x1, local copies, waits for them, and re-layouts  1.67 us

profile of v1, /device:TPU:0, one launch (start us, length us, event | category | flops | bytes accessed | tf_op | source)
XLA Modules:
  0.0 31.8 jit_solution(6592369477662227863)
XLA Ops:
  0.7 29.5 %shard_map.91 = f32[256,256]{1,0:T(8,128)} custom-call(s32[1,1]{1,0:T(1,128)S(6)} %copy.11.off_ref, bf16[384,256]{1,0:T(8,128)(2,1)} %f_ref.1, s32[384,256]{1,0:T(8,128)} %m_ref.1, f32[2,2,256,256]{3,2,1,0:T(8,128)} %constant.12.clone.fwd_hbm, f32[2,2,256,256]{3,2,1,0:T(8,128)} %constant.13.clone.inv_hbm, f32[256,256]{1,0:T(8,128)} %constant.14.clone.loc_ref, ...), custom_call_target="tpu_custom_call" | custom-call | tf_op jit(solution)/shard_map/pallas_call | solution.py:218
  30.1 1.7 %copy.12 = f32[256,256]{1,0:T(8,128)} copy(f32[256,256]{1,0:T(8,128)} %shard_map.91) | data formatting | bytes 524288

commit v2 on v1

v2 whole, which is shorter than its diff:
```python
import functools
import math

import jax
import jax.numpy as jnp
import numpy as np
from jax import lax
from jax.experimental import pallas as pl
from jax.experimental.pallas import tpu as pltpu
from jax.sharding import PartitionSpec as P

MARGIN = 128
MESH = pl.DeviceIdType.MESH
HIGHEST = lax.Precision.HIGHEST


def cosine_matrix(length):
    k = np.arange(length)[:, None]
    i = np.arange(length)[None, :]
    table = np.cos(np.pi * (((2 * i + 1) * k) % (4 * length)) / (2 * length))
    table *= np.where(k == 0, math.sqrt(1.0 / length), math.sqrt(2.0 / length))
    return table


def make_tables(n, tile_cols, n_rows, n_cols):
    strip_cols = n_cols * tile_cols
    screen = 16.0 / (tile_cols * tile_cols)
    full = cosine_matrix(strip_cols)
    blocks = full.reshape(n_cols, tile_cols, n_cols, tile_cols)
    inverse = blocks.transpose(2, 0, 1, 3)
    forward = blocks.transpose(0, 2, 3, 1)
    local = cosine_matrix(n)
    row_eigen = 4.0 * np.sin(np.pi * np.arange(n) / (2 * n)) ** 2
    col_eigen = 4.0 * np.sin(np.pi * np.arange(strip_cols) / (2 * strip_cols)) ** 2
    mu = screen + col_eigen
    theta = 2.0 * np.arcsinh(np.sqrt(mu) / 2.0)
    edge = np.exp(-theta) / (2.0 * np.sinh(theta))
    q = np.exp(-n * theta)
    params = np.zeros((n_cols, 8, tile_cols))
    params[:, 0] = theta.reshape(n_cols, tile_cols)
    params[:, 1] = (n * theta).reshape(n_cols, tile_cols)
    params[:, 2] = (edge / (1.0 - q ** (2 * n_rows))).reshape(n_cols, tile_cols)
    params[:, 3] = (edge / (1.0 - q * q)).reshape(n_cols, tile_cols)
    params[:, 4] = (edge * q / (1.0 - q * q)).reshape(n_cols, tile_cols)
    params[:, 5] = mu.reshape(n_cols, tile_cols)
    eigen = np.broadcast_to(row_eigen[:, None], (n, 128))
    both = np.stack([local, local.T])
    return [np.ascontiguousarray(t, dtype=np.float32) for t in (forward, inverse, both, eigen, params)]


CHUNKS = 4
LAG = 8


def exact(left, right):
    return jnp.dot(left, right, precision=HIGHEST, preferred_element_type=jnp.float32)


def kernel(
    n_rows, n_cols, off_ref, f_hbm, m_hbm, fwd_hbm, inv_hbm, loc_hbm, eig_hbm, par_hbm,
    out_ref, f_ref, m_ref, fwd, inv, loc, eig_ref, par_ref,
    spill_out, spill_in, own, xs, spec, ys, mom, weigh, coef, wave_f, wave_b,
    tab_sem, spill_send, spill_recv, x_send, x_recv, y_send, y_recv, m_send, m_recv, c_send, c_recv,
):
    a = lax.axis_index("rows")
    b = lax.axis_index("cols")
    n, w = out_ref.shape
    step = n // CHUNKS
    screen = 16.0 / (w * w)
    f32 = jnp.float32

    def load(k, src, dst):
        copy = pltpu.make_async_copy(src, dst, tab_sem.at[k])
        copy.start()
        return copy

    load_m = load(0, m_hbm, m_ref)
    load_f = load(1, f_hbm, f_ref)
    barrier = pltpu.get_barrier_semaphore()
    for k in range(1, n_rows):
        pl.semaphore_signal(barrier, inc=1, device_id={"rows": lax.rem(a + k, n_rows)}, device_id_type=MESH)
    for k in range(1, n_cols):
        pl.semaphore_signal(barrier, inc=1, device_id={"cols": lax.rem(b + k, n_cols)}, device_id_type=MESH)
    load_par = load(2, par_hbm, par_ref)
    load_fwd = load(3, fwd_hbm.at[b], fwd)
    load_loc = load(4, loc_hbm, loc)
    load_eig = load(5, eig_hbm, eig_ref)
    load_inv = load(6, inv_hbm.at[b], inv)

    s = off_ref[0, 0]

    def placing(first_row, count, first_t):
        r_at = lax.broadcasted_iota(jnp.int32, (count, n), 0) + first_row
        t_at = lax.broadcasted_iota(jnp.int32, (count, n), 1) + (first_t + s)
        return jnp.where(r_at == t_at, 1.0, 0.0).astype(jnp.bfloat16)

    def placed(matrix, pair):
        return jnp.dot(matrix, pair, preferred_element_type=f32)

    def pair_of(start):
        rows = pl.ds(start, n)
        return jnp.concatenate(
            [f_ref[rows, :], m_ref[rows, :].astype(f32).astype(jnp.bfloat16)], axis=1
        )

    first = placing(n - 2 * LAG, step + 2 * LAG, MARGIN)
    load_m.wait()
    load_f.wait()
    pair_low = pair_of(MARGIN)
    block = placed(first, pair_low)
    end_f, end_m = block[2 * LAG - 1 : 2 * LAG, :w], block[2 * LAG - 1 : 2 * LAG, w:]
    g_end = end_m * (block[2 * LAG : 2 * LAG + 1, :w] - end_f) / jnp.maximum(end_m, 1.0)
    spill_out[:LAG, :w] = jnp.broadcast_to(g_end, (LAG, w))
    spill_out[:LAG, w:] = jnp.zeros((LAG, w), f32)
    spill_out[LAG : LAG + step, :] = block[2 * LAG :]
    own[n : n + LAG, :] = block[2 * LAG : 3 * LAG]

    pl.semaphore_wait(barrier, n_rows - 1 + n_cols - 1)
    spill_copies = []
    for c in range(CHUNKS):
        lo = 0 if c == 0 else LAG + c * step
        rows = pl.ds(lo, LAG + (c + 1) * step - lo)
        if c > 0:
            spill_out[rows, :] = placed(placing(n + c * step, step, MARGIN), pair_low)
        spill_copies.append(
            pltpu.make_async_remote_copy(
                src_ref=spill_out.at[rows], dst_ref=spill_in.at[rows],
                send_sem=spill_send.at[c], recv_sem=spill_recv.at[c],
                device_id={"rows": lax.rem(a + 1, n_rows)}, device_id_type=MESH,
            )
        )
        pl.when(a < n_rows - 1)(spill_copies[-1].start)

    own[:n, :] = placed(placing(0, n, 0), pair_of(0))
    load_par.wait()
    row_f = lax.broadcasted_iota(jnp.int32, (n, w), 0).astype(f32)
    for c in range(n_cols):
        theta = par_ref[c, 0:1]
        wave_b[c] = jnp.exp(-theta * row_f)
        wave_f[c] = jnp.exp(-theta * ((n - 1) - row_f))
    n_theta = par_ref[b, 1:2]
    wide_edge = par_ref[b, 2:3]
    tile_edge = par_ref[b, 3:4]
    tile_edge_q = par_ref[b, 4:5]
    mu = par_ref[b, 5:6]
    period = 2 * n_rows

    def weight(power):
        return wide_edge * jnp.exp(-n_theta * power.astype(f32))

    for other in range(n_rows):
        weigh[0, other] = jnp.concatenate(
            [weight(lax.rem(a - 1 - other + period, period)), weight(a + other)], axis=1
        )
        weigh[1, other] = jnp.concatenate(
            [weight(period - 2 - a - other), weight(lax.rem(other - a - 1 + period, period))], axis=1
        )
    load_fwd.wait()
    spill_in[LAG + n :, :] = jnp.zeros((LAG, 2 * w), f32)

    @pl.when(a == 0)
    def _():
        spill_in[: LAG + n, :] = jnp.zeros((LAG + n, 2 * w), f32)

    def swap(buf, rows, send, recv, c):
        copies = []
        for k in range(1, n_cols):
            copies.append(
                pltpu.make_async_remote_copy(
                    src_ref=buf.at[b, rows], dst_ref=buf.at[b, rows],
                    send_sem=send.at[k, c], recv_sem=recv.at[k, c],
                    device_id={"cols": lax.rem(b + k, n_cols)}, device_id_type=MESH,
                )
            )
            copies[-1].start()
        return copies

    bounds = [0] + [c * step - LAG for c in range(1, CHUNKS)] + [n]
    mom_f = jnp.zeros((1, w), f32)
    mom_b = jnp.zeros((1, w), f32)
    gx_last = None
    swaps = []

    def transform(c, mom_f, mom_b):
        lo, hi = bounds[c], bounds[c + 1]
        total = exact(xs[b, lo:hi], fwd[b])
        for k in range(1, n_cols):
            swaps[c][k - 1].wait_recv()
            at = lax.rem(b + n_cols - k, n_cols)
            total += exact(xs[at, lo:hi], fwd[at])
        spec[lo:hi, :] = total
        mom_f += jnp.sum(wave_f[b, lo:hi] * total, axis=0, keepdims=True)
        mom_b += jnp.sum(wave_b[b, lo:hi] * total, axis=0, keepdims=True)
        return mom_f, mom_b

    for c in range(CHUNKS):
        lo, hi = bounds[c], bounds[c + 1]
        count = hi - lo
        pl.when(a > 0)(spill_copies[c].wait_recv)
        row_at = lax.broadcasted_iota(jnp.int32, (count, w), 0)
        col_at = lax.broadcasted_iota(jnp.int32, (count, w), 1)
        last_col = col_at == w - 1
        f1, m1 = own[lo:hi, :w], own[lo:hi, w:]
        f2, m2 = spill_in[LAG + lo : LAG + hi, :w], spill_in[LAG + lo : LAG + hi, w:]
        down1 = own[lo + 1 : hi + 1, :w] - f1
        under = spill_in[LAG + lo + 1 : LAG + hi + 1, :]
        down2 = jnp.where(under[:, w:] > 0.0, under[:, :w] - f2, 0.0)
        across1 = jnp.where(last_col, 0.0, pltpu.roll(f1, w - 1, 1) - f1)
        across2 = jnp.where(last_col, 0.0, pltpu.roll(f2, w - 1, 1) - f2)
        scale = 1.0 / jnp.maximum(m1 + m2, 1.0)
        composite = (m1 * f1 + m2 * f2) * scale
        gx = (m1 * down1 + m2 * down2) * scale
        if c == CHUNKS - 1:
            gx = jnp.where((row_at == count - 1) & (a == n_rows - 1), 0.0, gx)
        gy = (m1 * across1 + m2 * across2) * scale
        before = spill_in[LAG - 1 : LAG, :w] if c == 0 else gx_last
        gx_before = jnp.where(row_at == 0, before, pltpu.roll(gx, 1, 0))
        gy_before = jnp.where(col_at == 0, 0.0, pltpu.roll(gy, 1, 1))
        gx_last = gx[count - 1 : count]
        xs[b, lo:hi] = screen * composite - ((gx - gx_before) + (gy - gy_before))
        swaps.append(swap(xs, pl.ds(lo, count), x_send, x_recv, c))
        if c > 0:
            mom_f, mom_b = transform(c - 1, mom_f, mom_b)
    mom_f, mom_b = transform(CHUNKS - 1, mom_f, mom_b)

    mom[a] = jnp.concatenate([mom_f, mom_b], axis=1)
    m_copies = []
    for k in range(1, n_rows):
        m_copies.append(
            pltpu.make_async_remote_copy(
                src_ref=mom.at[a], dst_ref=mom.at[a], send_sem=m_send.at[k], recv_sem=m_recv.at[k],
                device_id={"rows": lax.rem(a + k, n_rows)}, device_id_type=MESH,
            )
        )
        m_copies[-1].start()
    load_loc.wait()
    load_eig.wait()
    eig = jnp.concatenate([eig_ref[...]] * (w // 128), axis=1)
    quotient = exact(loc[0], spec[...]) / (eig + mu)
    ys[b] = exact(loc[1], quotient)
    swaps.append(swap(ys, pl.ds(0, n), y_send, y_recv, 0))
    load_inv.wait()
    for copy in m_copies:
        copy.wait_recv()
    top = jnp.zeros((1, 2 * w), f32)
    bottom = jnp.zeros((1, 2 * w), f32)
    for other in range(n_rows):
        top += weigh[0, other] * mom[other]
        bottom += weigh[1, other] * mom[other]
    from_top = top[:, :w] + top[:, w:] - (tile_edge * mom_b + tile_edge_q * mom_f)
    from_bottom = bottom[:, :w] + bottom[:, w:] - (tile_edge * mom_f + tile_edge_q * mom_b)
    coef[b] = jnp.concatenate([from_top, from_bottom], axis=1)
    swaps.append(swap(coef, pl.ds(0, 1), c_send, c_recv, 0))

    def part(at):
        pair = coef[at]
        return exact(ys[at] + wave_b[at] * pair[:, :w] + wave_f[at] * pair[:, w:], inv[at])

    total = part(b)
    for k in range(1, n_cols):
        swaps[-2][k - 1].wait_recv()
        swaps[-1][k - 1].wait_recv()
        total += part(lax.rem(b + n_cols - k, n_cols))
    out_ref[...] = total

    for copies in swaps + [m_copies]:
        for copy in copies:
            copy.wait_send()
    for copy in spill_copies:
        pl.when(a < n_rows - 1)(copy.wait_send)


def shards(n_rows, n_cols, fields, masks, offsets):
    height, w = fields.shape
    n = height - MARGIN
    tables = make_tables(n, w, n_rows, n_cols)
    vmem = pl.BlockSpec(memory_space=pltpu.VMEM)
    anywhere = pl.BlockSpec(memory_space=pl.ANY)
    f32 = jnp.float32
    dma = pltpu.SemaphoreType.DMA
    return pl.pallas_call(
        functools.partial(kernel, n_rows, n_cols),
        out_shape=jax.ShapeDtypeStruct((n, w), f32),
        in_specs=[pl.BlockSpec(memory_space=pltpu.SMEM)] + [anywhere] * 7,
        out_specs=vmem,
        scratch_shapes=[
            pltpu.VMEM((height, w), fields.dtype),
            pltpu.VMEM((height, w), masks.dtype),
            pltpu.VMEM((n_cols, w, w), f32),
            pltpu.VMEM((n_cols, w, w), f32),
            pltpu.VMEM((2, n, n), f32),
            pltpu.VMEM((n, 128), f32),
            pltpu.VMEM((n_cols, 8, w), f32),
            pltpu.VMEM((n + LAG, 2 * w), f32),
            pltpu.VMEM((n + 2 * LAG, 2 * w), f32),
            pltpu.VMEM((n + LAG, 2 * w), f32),
            pltpu.VMEM((n_cols, n, w), f32),
            pltpu.VMEM((n, w), f32),
            pltpu.VMEM((n_cols, n, w), f32),
            pltpu.VMEM((n_rows, 1, 2 * w), f32),
            pltpu.VMEM((2, n_rows, 1, 2 * w), f32),
            pltpu.VMEM((n_cols, 1, 2 * w), f32),
            pltpu.VMEM((n_cols, n, w), f32),
            pltpu.VMEM((n_cols, n, w), f32),
            dma((7,)),
            dma((CHUNKS,)),
            dma((CHUNKS,)),
            dma((n_cols, CHUNKS)),
            dma((n_cols, CHUNKS)),
            dma((n_cols, 1)),
            dma((n_cols, 1)),
            dma((n_rows,)),
            dma((n_rows,)),
            dma((n_cols, 1)),
            dma((n_cols, 1)),
        ],
        compiler_params=pltpu.CompilerParams(
            collective_id=0, has_side_effects=True, vmem_limit_bytes=56 * 1024 * 1024
        ),
    )(offsets, fields, masks, *tables)


def solution(mesh):
    placed = (P("rows", "cols"), P("rows", "cols"), P("rows", "cols"))
    body = functools.partial(shards, mesh.shape["rows"], mesh.shape["cols"])
    return jax.shard_map(body, mesh=mesh, in_specs=placed, out_specs=P("rows", "cols"), check_vma=False)
```

time: 32 us -> 30 us (0.938)
  Pallas kernels: 29.5 us -> 27.4 us
    pallas_call x1, Pallas kernels: 29.5 us -> 27.4 us  [shards(): pl.pallas_call(functools.partial(kernel, n_rows, n_cols), out_shape=jax.S...]
where the time goes in v2:
time: 30 us; the launch traced here: 29.7 us
  Pallas kernels  27.4 us (91%)
  local copies, waits for them, and re-layouts  1.67 us (6%)
  between operations  0.66 us (2%)
    pallas_call x1, Pallas kernels, shards(): pl.pallas_call(functools.partial(kernel, n_rows, n_cols), out_shape=jax.S...  27.4 us
    unnamed x1, local copies, waits for them, and re-layouts  1.67 us

profile of v2, /device:TPU:0, one launch (start us, length us, event | category | flops | bytes accessed | tf_op | source)
XLA Modules:
  0.0 29.7 jit_solution(14181482282326713661)
XLA Ops:
  0.7 27.4 %shard_map.82 = f32[256,256]{1,0:T(8,128)} custom-call(s32[1,1]{1,0:T(1,128)S(6)} %copy.10.off_ref, bf16[384,256]{1,0:T(8,128)(2,1)} %f_hbm.1, s32[384,256]{1,0:T(8,128)} %m_hbm.1, f32[2,2,256,256]{3,2,1,0:T(8,128)} %constant.10.clone.fwd_hbm, f32[2,2,256,256]{3,2,1,0:T(8,128)} %constant.11.clone.inv_hbm, f32[2,256,256]{2,1,0:T(8,128)} %constant.12.clone.loc_hbm, ...), custom_call_target="tpu_custom_call" | custom-call | tf_op jit(solution)/shard_map/pallas_call | solution.py:281
  28.0 1.7 %copy.11 = f32[256,256]{1,0:T(8,128)} copy(f32[256,256]{1,0:T(8,128)} %shard_map.82) | data formatting | bytes 524288

commit v3 on v2

--- a/solution.py
+++ b/solution.py
@@ -28,7 +28,11 @@
     full = cosine_matrix(strip_cols)
     blocks = full.reshape(n_cols, tile_cols, n_cols, tile_cols)
     inverse = blocks.transpose(2, 0, 1, 3)
-    forward = blocks.transpose(0, 2, 3, 1)
+    forward = blocks.transpose(2, 0, 3, 1)
+    inverse = inverse.astype(np.float32)
+    high = inverse.astype(jnp.bfloat16)
+    low = (inverse - high.astype(np.float32)).astype(jnp.bfloat16)
+    inverse = np.stack([high, low], axis=2)
     local = cosine_matrix(n)
     row_eigen = 4.0 * np.sin(np.pi * np.arange(n) / (2 * n)) ** 2
     col_eigen = 4.0 * np.sin(np.pi * np.arange(strip_cols) / (2 * strip_cols)) ** 2
@@ -45,7 +49,10 @@
     params[:, 5] = mu.reshape(n_cols, tile_cols)
     eigen = np.broadcast_to(row_eigen[:, None], (n, 128))
     both = np.stack([local, local.T])
-    return [np.ascontiguousarray(t, dtype=np.float32) for t in (forward, inverse, both, eigen, params)]
+    forward, both, eigen, params = [
+        np.ascontiguousarray(t, dtype=np.float32) for t in (forward, both, eigen, params)
+    ]
+    return forward, inverse, both, eigen, params
 
 
 CHUNKS = 4
@@ -56,10 +63,20 @@
     return jnp.dot(left, right, precision=HIGHEST, preferred_element_type=jnp.float32)
 
 
+def three_pass(left, right):
+    high = left.astype(jnp.bfloat16)
+    low = (left - high.astype(jnp.float32)).astype(jnp.bfloat16)
+
+    def product(x, y):
+        return jnp.dot(x, y, preferred_element_type=jnp.float32)
+
+    return product(high, right[0]) + (product(low, right[0]) + product(high, right[1]))
+
+
 def kernel(
     n_rows, n_cols, off_ref, f_hbm, m_hbm, fwd_hbm, inv_hbm, loc_hbm, eig_hbm, par_hbm,
-    out_ref, f_ref, m_ref, fwd, inv, loc, eig_ref, par_ref,
-    spill_out, spill_in, own, xs, spec, ys, mom, weigh, coef, wave_f, wave_b,
+    out_ref, rest_ref, f_ref, m_ref, fwd, inv, loc, eig_ref, par_ref,
+    spill_out, spill_in, own, mine, theirs, ys, mom, sums, weigh, wave_f, wave_b,
     tab_sem, spill_send, spill_recv, x_send, x_recv, y_send, y_recv, m_send, m_recv, c_send, c_recv,
 ):
     a = lax.axis_index("rows")
@@ -138,11 +155,12 @@
         theta = par_ref[c, 0:1]
         wave_b[c] = jnp.exp(-theta * row_f)
         wave_f[c] = jnp.exp(-theta * ((n - 1) - row_f))
-    n_theta = par_ref[b, 1:2]
-    wide_edge = par_ref[b, 2:3]
-    tile_edge = par_ref[b, 3:4]
-    tile_edge_q = par_ref[b, 4:5]
     mu = par_ref[b, 5:6]
+
+    def all_waves(row):
+        return jnp.concatenate([par_ref[c, row : row + 1] for c in range(n_cols)], axis=1)
+
+    n_theta, wide_edge, tile_edge, tile_edge_q = [all_waves(row) for row in (1, 2, 3, 4)]
     period = 2 * n_rows
 
     def weight(power):
@@ -162,36 +180,24 @@
     def _():
         spill_in[: LAG + n, :] = jnp.zeros((LAG + n, 2 * w), f32)
 
-    def swap(buf, rows, send, recv, c):
+    def swap(source, target, send, recv, c):
         copies = []
         for k in range(1, n_cols):
+            to = lax.rem(b + k, n_cols)
             copies.append(
                 pltpu.make_async_remote_copy(
-                    src_ref=buf.at[b, rows], dst_ref=buf.at[b, rows],
-                    send_sem=send.at[k, c], recv_sem=recv.at[k, c],
-                    device_id={"cols": lax.rem(b + k, n_cols)}, device_id_type=MESH,
+                    src_ref=source(to), dst_ref=target, send_sem=send.at[k, c], recv_sem=recv.at[k, c],
+                    device_id={"cols": to}, device_id_type=MESH,
                 )
             )
             copies[-1].start()
         return copies
 
     bounds = [0] + [c * step - LAG for c in range(1, CHUNKS)] + [n]
-    mom_f = jnp.zeros((1, w), f32)
-    mom_b = jnp.zeros((1, w), f32)
+    mom_f = [jnp.zeros((1, w), f32)] * n_cols
+    mom_b = [jnp.zeros((1, w), f32)] * n_cols
     gx_last = None
     swaps = []
-
-    def transform(c, mom_f, mom_b):
-        lo, hi = bounds[c], bounds[c + 1]
-        total = exact(xs[b, lo:hi], fwd[b])
-        for k in range(1, n_cols):
-            swaps[c][k - 1].wait_recv()
-            at = lax.rem(b + n_cols - k, n_cols)
-            total += exact(xs[at, lo:hi], fwd[at])
-        spec[lo:hi, :] = total
-        mom_f += jnp.sum(wave_f[b, lo:hi] * total, axis=0, keepdims=True)
-        mom_b += jnp.sum(wave_b[b, lo:hi] * total, axis=0, keepdims=True)
-        return mom_f, mom_b
 
     for c in range(CHUNKS):
         lo, hi = bounds[c], bounds[c + 1]
@@ -217,13 +223,26 @@
         gx_before = jnp.where(row_at == 0, before, pltpu.roll(gx, 1, 0))
         gy_before = jnp.where(col_at == 0, 0.0, pltpu.roll(gy, 1, 1))
         gx_last = gx[count - 1 : count]
-        xs[b, lo:hi] = screen * composite - ((gx - gx_before) + (gy - gy_before))
-        swaps.append(swap(xs, pl.ds(lo, count), x_send, x_recv, c))
-        if c > 0:
-            mom_f, mom_b = transform(c - 1, mom_f, mom_b)
-    mom_f, mom_b = transform(CHUNKS - 1, mom_f, mom_b)
-
-    mom[a] = jnp.concatenate([mom_f, mom_b], axis=1)
+        right_side = screen * composite - ((gx - gx_before) + (gy - gy_before))
+        for waves in range(n_cols):
+            partial = exact(right_side, fwd[waves])
+            mine[waves, lo:hi] = partial
+            mom_f[waves] += jnp.sum(wave_f[waves, lo:hi] * partial, axis=0, keepdims=True)
+            mom_b[waves] += jnp.sum(wave_b[waves, lo:hi] * partial, axis=0, keepdims=True)
+        if c < CHUNKS - 1:
+            rows = pl.ds(lo, count)
+            swaps.append(swap(lambda to: mine.at[to, rows], theirs.at[b, rows], x_send, x_recv, c))
+
+    sums[b] = jnp.concatenate(mom_f + mom_b, axis=1)
+    sum_copies = swap(lambda to: sums.at[b], sums.at[b], c_send, c_recv, 0)
+    rows = pl.ds(lo, count)
+    swaps.append(swap(lambda to: mine.at[to, rows], theirs.at[b, rows], x_send, x_recv, CHUNKS - 1))
+    for copy in sum_copies:
+        copy.wait_recv()
+    tile_sums = sums[0]
+    for c in range(1, n_cols):
+        tile_sums += sums[c]
+    mom[a] = tile_sums
     m_copies = []
     for k in range(1, n_rows):
         m_copies.append(
@@ -235,35 +254,40 @@
         m_copies[-1].start()
     load_loc.wait()
     load_eig.wait()
+    for copies in swaps:
+        for copy in copies:
+            copy.wait_recv()
+    spectral = mine[b]
+    for k in range(1, n_cols):
+        spectral += theirs[lax.rem(b + k, n_cols)]
     eig = jnp.concatenate([eig_ref[...]] * (w // 128), axis=1)
-    quotient = exact(loc[0], spec[...]) / (eig + mu)
+    quotient = exact(loc[0], spectral) / (eig + mu)
     ys[b] = exact(loc[1], quotient)
-    swaps.append(swap(ys, pl.ds(0, n), y_send, y_recv, 0))
+    y_copies = swap(lambda to: ys.at[b], ys.at[b], y_send, y_recv, 0)
     load_inv.wait()
-    for copy in m_copies:
+    for copy in y_copies + m_copies:
         copy.wait_recv()
-    top = jnp.zeros((1, 2 * w), f32)
-    bottom = jnp.zeros((1, 2 * w), f32)
+    top = jnp.zeros_like(tile_sums)
+    bottom = jnp.zeros_like(tile_sums)
     for other in range(n_rows):
         top += weigh[0, other] * mom[other]
         bottom += weigh[1, other] * mom[other]
-    from_top = top[:, :w] + top[:, w:] - (tile_edge * mom_b + tile_edge_q * mom_f)
-    from_bottom = bottom[:, :w] + bottom[:, w:] - (tile_edge * mom_f + tile_edge_q * mom_b)
-    coef[b] = jnp.concatenate([from_top, from_bottom], axis=1)
-    swaps.append(swap(coef, pl.ds(0, 1), c_send, c_recv, 0))
-
-    def part(at):
-        pair = coef[at]
-        return exact(ys[at] + wave_b[at] * pair[:, :w] + wave_f[at] * pair[:, w:], inv[at])
-
-    total = part(b)
-    for k in range(1, n_cols):
-        swaps[-2][k - 1].wait_recv()
-        swaps[-1][k - 1].wait_recv()
-        total += part(lax.rem(b + n_cols - k, n_cols))
-    out_ref[...] = total
-
-    for copies in swaps + [m_copies]:
+    width = n_cols * w
+    own_f, own_b = tile_sums[:, :width], tile_sums[:, width:]
+    from_top = top[:, :width] + top[:, width:] - (tile_edge * own_b + tile_edge_q * own_f)
+    from_bottom = bottom[:, :width] + bottom[:, width:] - (tile_edge * own_f + tile_edge_q * own_b)
+
+    def part(c):
+        at = slice(c * w, (c + 1) * w)
+        return three_pass(ys[c] + wave_b[c] * from_top[:, at] + wave_f[c] * from_bottom[:, at], inv[c])
+
+    out_ref[...] = part(0)
+    rest = jnp.zeros((n, w), f32)
+    for c in range(1, n_cols):
+        rest += part(c)
+    rest_ref[...] = rest
+
+    for copies in swaps + [sum_copies, y_copies, m_copies]:
         for copy in copies:
             copy.wait_send()
     for copy in spill_copies:
@@ -278,16 +302,16 @@
     anywhere = pl.BlockSpec(memory_space=pl.ANY)
     f32 = jnp.float32
     dma = pltpu.SemaphoreType.DMA
-    return pl.pallas_call(
+    out, rest = pl.pallas_call(
         functools.partial(kernel, n_rows, n_cols),
-        out_shape=jax.ShapeDtypeStruct((n, w), f32),
+        out_shape=[jax.ShapeDtypeStruct((n, w), f32)] * 2,
         in_specs=[pl.BlockSpec(memory_space=pltpu.SMEM)] + [anywhere] * 7,
-        out_specs=vmem,
+        out_specs=[vmem] * 2,
         scratch_shapes=[
             pltpu.VMEM((height, w), fields.dtype),
             pltpu.VMEM((height, w), masks.dtype),
             pltpu.VMEM((n_cols, w, w), f32),
-            pltpu.VMEM((n_cols, w, w), f32),
+            pltpu.VMEM((n_cols, 2, w, w), jnp.bfloat16),
             pltpu.VMEM((2, n, n), f32),
             pltpu.VMEM((n, 128), f32),
             pltpu.VMEM((n_cols, 8, w), f32),
@@ -295,11 +319,11 @@
             pltpu.VMEM((n + 2 * LAG, 2 * w), f32),
             pltpu.VMEM((n + LAG, 2 * w), f32),
             pltpu.VMEM((n_cols, n, w), f32),
-            pltpu.VMEM((n, w), f32),
-            pltpu.VMEM((n_cols, n, w), f32),
-            pltpu.VMEM((n_rows, 1, 2 * w), f32),
-            pltpu.VMEM((2, n_rows, 1, 2 * w), f32),
-            pltpu.VMEM((n_cols, 1, 2 * w), f32),
+            pltpu.VMEM((n_cols, n, w), f32),
+            pltpu.VMEM((n_cols, n, w), f32),
+            pltpu.VMEM((n_rows, 1, 2 * n_cols * w), f32),
+            pltpu.VMEM((n_cols, 1, 2 * n_cols * w), f32),
+            pltpu.VMEM((2, n_rows, 1, 2 * n_cols * w), f32),
             pltpu.VMEM((n_cols, n, w), f32),
             pltpu.VMEM((n_cols, n, w), f32),
             dma((7,)),
@@ -315,9 +339,10 @@
             dma((n_cols, 1)),
         ],
         compiler_params=pltpu.CompilerParams(
-            collective_id=0, has_side_effects=True, vmem_limit_bytes=56 * 1024 * 1024
+            collective_id=0, has_side_effects=True, vmem_limit_bytes=40 * 1024 * 1024
         ),
     )(offsets, fields, masks, *tables)
+    return out + rest
 
 
 def solution(mesh):

time: 30 us -> 34 us (1.13)
  local copies, waits for them, and re-layouts: 1.67 us -> 7.03 us
  Pallas kernels: 27.4 us -> 25.2 us
  other arithmetic: 0 us -> 0.74 us
    unnamed x1 -> x14, local copies, waits for them, and re-layouts: 1.67 us -> 7.03 us
    pallas_call x1, Pallas kernels: 27.4 us -> 25.2 us  [shards(): pl.pallas_call(functools.partial(kernel, n_rows, n_cols), out_shape=[jax....]
    add x0 -> x1, other arithmetic: none -> 0.74 us  [shards(): return out + rest]
where the time goes in v3:
time: 34 us; the launch traced here: 33.6 us
  Pallas kernels  25.2 us (74%)
  local copies, waits for them, and re-layouts  7.03 us (21%)
  other arithmetic  0.74 us (2%)
  between operations  0.67 us (2%)
    pallas_call x1, Pallas kernels, shards(): pl.pallas_call(functools.partial(kernel, n_rows, n_cols), out_shape=[jax....  25.2 us
    unnamed x14, local copies, waits for them, and re-layouts  7.03 us
    add x1, other arithmetic, shards(): return out + rest  0.74 us

profile of v3, /device:TPU:0, one launch (start us, length us, event | category | flops | bytes accessed | tf_op | source)
XLA Modules:
  0.0 33.6 jit_solution(9159178784335480645)
XLA Ops:
  0.7 0.0 copy-start
  0.7 1.2 %copy-done = bf16[2,2,2,256,256]{4,3,2,1,0:T(8,128)(2,1)S(1)} copy-done((bf16[2,2,2,256,256]{4,3,2,1,0:T(8,128)(2,1)S(1)}, bf16[2,2,2,256,256]{4,3,2,1,0:T(8,128)(2,1)}, u32[]{:S(2)}) %copy-start) | copy-done | bytes 1048600
  1.9 0.0 copy-start.1
  1.9 1.2 %copy-done.1 = f32[2,2,256,256]{3,2,1,0:T(8,128)S(1)} copy-done((f32[2,2,256,256]{3,2,1,0:T(8,128)S(1)}, f32[2,2,256,256]{3,2,1,0:T(8,128)}, u32[]{:S(2)}) %copy-start.1) | copy-done | bytes 1048600
  3.1 0.0 copy-start.2
  3.1 1.0 %copy-done.2 = f32[2,256,256]{2,1,0:T(8,128)S(1)} copy-done((f32[2,256,256]{2,1,0:T(8,128)S(1)}, f32[2,256,256]{2,1,0:T(8,128)}, u32[]{:S(2)}) %copy-start.2) | copy-done | bytes 524312
  4.1 0.0 copy-start.3
  4.2 1.0 %copy-done.3 = s32[384,256]{1,0:T(8,128)S(1)} copy-done((s32[384,256]{1,0:T(8,128)S(1)}, s32[384,256]{1,0:T(8,128)}, u32[]{:S(2)}) %copy-start.3) | copy-done | bytes 393240
  5.1 0.0 copy-start.4
  5.1 0.9 %copy-done.4 = bf16[384,256]{1,0:T(8,128)(2,1)S(1)} copy-done((bf16[384,256]{1,0:T(8,128)(2,1)S(1)}, bf16[384,256]{1,0:T(8,128)(2,1)}, u32[]{:S(2)}) %copy-start.4) | copy-done | bytes 196632
  6.1 0.0 copy-start.5
  6.1 0.9 %copy-done.5 = f32[256,128]{1,0:T(8,128)S(1)} copy-done((f32[256,128]{1,0:T(8,128)S(1)}, f32[256,128]{1,0:T(8,128)}, u32[]{:S(2)}) %copy-start.5) | copy-done | bytes 131096
  7.0 0.0 copy-start.6
  7.0 0.7 %copy-done.6 = f32[2,8,256]{2,1,0:T(8,128)S(1)} copy-done((f32[2,8,256]{2,1,0:T(8,128)S(1)}, f32[2,8,256]{2,1,0:T(8,128)}, u32[]{:S(2)}) %copy-start.6) | copy-done | bytes 16408
  7.7 25.2 %shard_map.82 = (f32[256,256]{1,0:T(8,128)S(1)}, f32[256,256]{1,0:T(8,128)S(1)}) custom-call(s32[1,1]{1,0:T(1,128)S(6)} %copy.9.off_ref, bf16[384,256]{1,0:T(8,128)(2,1)S(1)} %copy-done.4, s32[384,256]{1,0:T(8,128)S(1)} %copy-done.3, f32[2,2,256,256]{3,2,1,0:T(8,128)S(1)} %copy-done.1, bf16[2,2,2,256,256]{4,3,2,1,0:T(8,128)(2,1)S(1)} %copy-done, ...), custom_call_target="tpu_custom_call" | custom-call | tf_op jit(solution)/shard_map/pallas_call | solution.py:305
  32.9 0.7 %add.3 = f32[256,256]{1,0:T(8,128)} add(f32[256,256]{1,0:T(8,128)S(1)} %get-tuple-element.7, f32[256,256]{1,0:T(8,128)S(1)} %get-tuple-element.8) | non-fusion elementwise | flops 65536 | bytes 786432 | tf_op jit(solution)/shard_map/add | solution.py:345
Async XLA Ops:
  0.7 1.2 %copy-start = (bf16[2,2,2,256,256]{4,3,2,1,0:T(8,128)(2,1)S(1)}, bf16[2,2,2,256,256]{4,3,2,1,0:T(8,128)(2,1)}, u32[]{:S(2)}) copy-start(bf16[2,2,2,256,256]{4,3,2,1,0:T(8,128)(2,1)} %constant.11.clone.inv_hbm) | copy-start | bytes 3145732
  1.9 1.2 %copy-start.1 = (f32[2,2,256,256]{3,2,1,0:T(8,128)S(1)}, f32[2,2,256,256]{3,2,1,0:T(8,128)}, u32[]{:S(2)}) copy-start(f32[2,2,256,256]{3,2,1,0:T(8,128)} %constant.10.clone.fwd_hbm) | copy-start | bytes 3145732
  3.1 1.0 %copy-start.2 = (f32[2,256,256]{2,1,0:T(8,128)S(1)}, f32[2,256,256]{2,1,0:T(8,128)}, u32[]{:S(2)}) copy-start(f32[2,256,256]{2,1,0:T(8,128)} %constant.12.clone.loc_hbm) | copy-start | bytes 1572868
  4.1 1.0 %copy-start.3 = (s32[384,256]{1,0:T(8,128)S(1)}, s32[384,256]{1,0:T(8,128)}, u32[]{:S(2)}) copy-start(s32[384,256]{1,0:T(8,128)} %m_hbm.1) | copy-start | bytes 1179652
  5.1 0.9 %copy-start.4 = (bf16[384,256]{1,0:T(8,128)(2,1)S(1)}, bf16[384,256]{1,0:T(8,128)(2,1)}, u32[]{:S(2)}) copy-start(bf16[384,256]{1,0:T(8,128)(2,1)} %f_hbm.1) | copy-start | bytes 589828
  6.1 0.9 %copy-start.5 = (f32[256,128]{1,0:T(8,128)S(1)}, f32[256,128]{1,0:T(8,128)}, u32[]{:S(2)}) copy-start(f32[256,128]{1,0:T(8,128)} %constant.13.clone.eig_hbm) | copy-start | bytes 393220
  7.0 0.7 %copy-start.6 = (f32[2,8,256]{2,1,0:T(8,128)S(1)}, f32[2,8,256]{2,1,0:T(8,128)}, u32[]{:S(2)}) copy-start(f32[2,8,256]{2,1,0:T(8,128)} %constant.14.clone.par_hbm) | copy-start | bytes 49156

commit v4 on v3

--- a/solution.py
+++ b/solution.py
@@ -339,7 +339,7 @@
             dma((n_cols, 1)),
         ],
         compiler_params=pltpu.CompilerParams(
-            collective_id=0, has_side_effects=True, vmem_limit_bytes=40 * 1024 * 1024
+            collective_id=0, has_side_effects=True, vmem_limit_bytes=56 * 1024 * 1024
         ),
     )(offsets, fields, masks, *tables)
     return out + rest

time: 34 us -> 28.1 us (0.83)
  local copies, waits for them, and re-layouts: 7.03 us -> 0 us
  other arithmetic: 0.74 us -> 1.77 us
  Pallas kernels: 25.2 us -> 25.6 us
    unnamed x14 -> x0, local copies, waits for them, and re-layouts: 7.03 us -> none
    add x1, other arithmetic: 0.74 us -> 1.77 us  [shards(): return out + rest]
    pallas_call x1, Pallas kernels: 25.2 us -> 25.6 us  [shards(): pl.pallas_call(functools.partial(kernel, n_rows, n_cols), out_shape=[jax....]
where the time goes in v4:
time: 28.1 us; the launch traced here: 28 us
  Pallas kernels  25.6 us (91%)
  other arithmetic  1.77 us (6%)
  between operations  0.66 us (2%)
    pallas_call x1, Pallas kernels, shards(): pl.pallas_call(functools.partial(kernel, n_rows, n_cols), out_shape=[jax....  25.6 us
    add x1, other arithmetic, shards(): return out + rest  1.77 us

profile of v4, /device:TPU:0, one launch (start us, length us, event | category | flops | bytes accessed | tf_op | source)
XLA Modules:
  0.0 28.0 jit_solution(9044911117570496095)
XLA Ops:
  0.7 25.6 %shard_map.82 = (f32[256,256]{1,0:T(8,128)}, f32[256,256]{1,0:T(8,128)}) custom-call(s32[1,1]{1,0:T(1,128)S(6)} %copy.9.off_ref, bf16[384,256]{1,0:T(8,128)(2,1)} %f_hbm.1, s32[384,256]{1,0:T(8,128)} %m_hbm.1, f32[2,2,256,256]{3,2,1,0:T(8,128)} %constant.10.clone.fwd_hbm, bf16[2,2,2,256,256]{4,3,2,1,0:T(8,128)(2,1)} %constant.11.clone.inv_hbm, ...), custom_call_target="tpu_custom_call" | custom-call | tf_op jit(solution)/shard_map/pallas_call | solution.py:305
  26.2 1.8 %add.3 = f32[256,256]{1,0:T(8,128)} add(f32[256,256]{1,0:T(8,128)} %get-tuple-element.7, f32[256,256]{1,0:T(8,128)} %get-tuple-element.8) | non-fusion elementwise | flops 65536 | bytes 786432 | tf_op jit(solution)/shard_map/add | solution.py:345
